TPU v7x, 256 devices: a whole 4x4x8 slice. The times are simulated.
256 devices in a mesh: seq: 32 (over z_lo, x, core), tp: 8 (over z_hi, y).
Axes of the slice: x: 4, y: 4, z: 8 (z_hi: 2, z_lo: 4; z = z_hi * 4 + z_lo), core: 2. Of those that a mesh axis runs over, the one named last changes fastest.
Arguments:
- tokens: bfloat16 [2048, 8192], P('seq', 'tp'), may hold values from -6 to 6
- out_grad: bfloat16 [2048, 8192], P('seq', 'tp'), may hold values from -6 to 6
- w_in: bfloat16 [8192, 16384], P('tp', 'seq'), may hold values from -0.0625 to 0.0625
- w_out: bfloat16 [16384, 8192], P('seq', 'tp'), may hold values from -0.046875 to 0.046875
- sketch: bfloat16 [2048, 256], P('seq'), may hold values from -0.375 to 0.375
Outputs:
- input_grad: bfloat16 [2048, 8192], P('seq', 'tp')
- grad_in: bfloat16 [8192, 16384], P('tp', 'seq')
- grad_out: bfloat16 [16384, 8192], P('seq', 'tp')
All inputs are finite; a program needn't handle non-finite values.
Results may differ from a plain program's by a relative error of at most 0.0063.
Values may be sent and summed in bfloat16 or wider, within the bound.
A program may use at most 128 MiB of HBM per device.

v0:
```python
import math

import jax
import jax.numpy as jnp
from jax import lax
from jax.sharding import PartitionSpec as P

inv_root_two = 0.7071067811865476
inv_root_twopi = 0.3989422804014327


def gelu_slope(values):
    return (
        0.5 * (1.0 + lax.erf(values * inv_root_two))
        + values * jnp.exp(-0.5 * values * values) * inv_root_twopi
    )


def local(tokens, out_grad, w_in, w_out, sketch):
    all_tokens, all_sketch = (
        lax.all_gather(tokens, "seq", axis=0, tiled=True),
        lax.all_gather(sketch, "seq", axis=0, tiled=True),
    )
    all_rows = all_tokens.shape[0]
    pre_act = lax.psum(jnp.dot(all_tokens, w_in, preferred_element_type=jnp.float32), "tp")
    hidden = jax.nn.gelu(pre_act, approximate=False).astype(jnp.bfloat16)
    all_grads = lax.all_gather(out_grad, "seq", axis=0, tiled=True)
    whole_term = jnp.einsum("td,fd->tf", all_grads, w_out, preferred_element_type=jnp.float32)
    d_hidden = lax.psum(whole_term, "tp")
    d_pre = (d_hidden * gelu_slope(pre_act)).astype(jnp.bfloat16)
    hidden_part = jnp.einsum("tr,tf->rf", all_sketch, hidden, preferred_element_type=jnp.float32)
    dpre_part = jnp.einsum("tr,tf->rf", all_sketch, d_pre, preferred_element_type=jnp.float32)
    sk_hidden = hidden_part.astype(jnp.bfloat16)
    sk_dpre = dpre_part.astype(jnp.bfloat16)
    partial_input = jnp.einsum("tf,df->td", d_pre, w_in, preferred_element_type=jnp.float32)
    input_grad = lax.psum_scatter(partial_input, "seq", scatter_dimension=0, tiled=True).astype(
        jnp.bfloat16
    )
    tokens_sum = jnp.einsum("tr,td->rd", all_sketch, all_tokens, preferred_element_type=jnp.float32)
    grads_sum = jnp.einsum("tr,td->rd", all_sketch, all_grads, preferred_element_type=jnp.float32)
    sk_tokens = tokens_sum.astype(jnp.bfloat16)
    sk_grads = grads_sum.astype(jnp.bfloat16)
    grad_scale = 1.0 / math.sqrt(all_rows)
    grad_in = (
        jnp.einsum("rd,rf->df", sk_tokens, sk_dpre, preferred_element_type=jnp.float32) * grad_scale
    ).astype(jnp.bfloat16)
    grad_out = (
        jnp.einsum("rf,rd->fd", sk_hidden, sk_grads, preferred_element_type=jnp.float32)
        * grad_scale
    ).astype(jnp.bfloat16)
    return (input_grad, grad_in, grad_out)


def solution(mesh):
    return jax.shard_map(
        local,
        mesh=mesh,
        in_specs=(P("seq", "tp"), P("seq", "tp"), P("tp", "seq"), P("seq", "tp"), P("seq", None)),
        out_specs=(P("seq", "tp"), P("tp", "seq"), P("seq", "tp")),
        check_vma=False,
    )
```

profile of v0, /device:TPU:8, one launch (start us, length us, event | category | flops | bytes accessed | tf_op | source)
XLA Modules:
  0.0 720.2 jit_solution(9599078181964682299)
XLA Ops:
  7.2 0.0 copy-start
  7.2 0.0 all-gather.4.cloned.1.call-start
  7.2 0.7 all-gather.4.cloned.1.call-update
  7.9 0.0 all-gather.6.cloned.1.call-start
  8.0 0.7 all-gather.6.cloned.1.call-update
  8.7 0.0 all-reduce.3.cloned.1.call-start
  8.7 66.9 %all-gather.4.cloned.1.call-done = bf16[2048,1024]{1,0:T(8,128)(2,1)} async-done(((bf16[64,1024]{1,0:T(8,128)(2,1)}), bf16[2048,1024]{1,0:T(8,128)(2,1)}) %all-gather.4.cloned.1.call-update) | async-done | bytes 4194320 | tf_op jit(solution)/shard_map/all_gather | solution.py:27
  75.6 6.8 fusion.51
  82.5 56.9 %all-gather.6.cloned.1.call-done = bf16[2048,1024]{1,0:T(8,128)(2,1)} async-done(((bf16[64,1024]{1,0:T(8,128)(2,1)}), bf16[2048,1024]{1,0:T(8,128)(2,1)}) %all-gather.6.cloned.1.call-update) | async-done | bytes 4194320 | tf_op jit(solution)/shard_map/all_gather | solution.py:21
  139.4 0.0 copy-done
  139.4 6.5 fusion.52
  145.9 0.0 all-reduce.3.cloned.1.call-update
  145.9 0.0 all-gather.8.cloned.1.call-start
  146.0 0.5 all-gather.8.cloned.1.call-update
  146.5 0.2 reduce-scatter.2.cloned.1.call-start
  146.7 338.2 %all-reduce.3.cloned.1.call-done = (f32[2048,512]{1,0:T(8,128)}, f32[2048,512]{1,0:T(8,128)}) async-done(((f32[2048,512]{1,0:T(8,128)}, f32[2048,512]{1,0:T(8,128)}), (f32[2048,512]{1,0:T(8,128)}, f32[2048,512]{1,0:T(8,128)})) %all-reduce.3.cloned.1.call-update) | async-done | bytes 8388624 | tf_op jit(solution)/shard_map/psum | solution.py:29
  484.9 4.3 fusion.5
  489.3 5.6 fusion.53
  494.9 0.0 reduce-scatter.2.cloned.1.call-update
  494.9 58.2 %all-gather.8.cloned.1.call-done = bf16[2048,256]{1,0:T(8,128)(2,1)} async-done(((bf16[64,256]{1,0:T(8,128)(2,1)}), bf16[2048,256]{1,0:T(8,128)(2,1)}) %all-gather.8.cloned.1.call-update) | async-done | bytes 1048592 | tf_op jit(solution)/shard_map/all_gather | solution.py:22
  553.1 2.0 convolution_convert_fusion.2
  555.1 0.0 copy-start.1
  555.1 5.2 multiply_convert_fusion.1
  560.4 0.0 copy-done.1
  560.4 10.9 %fusion.18 = bf16[512,256]{1,0:T(8,128)(2,1)S(1)} fusion(bf16[2048,256]{1,0:T(8,128)(2,1)S(1)} %copy-done.1, f32[2048,512]{1,0:T(8,128)} %get-tuple-element.4), kind=kOutput, calls=%fused_computation.32 | convolution fusion | flops 605159424 | bytes 5505024 | tf_op jit(solution)/shard_map/tr,tf->rf/dot_general | solution.py:31
  571.3 4.8 multiply_convert_fusion
  576.0 136.0 %reduce-scatter.2.cloned.1.call-done = f32[64,1024]{1,0:T(8,128)} async-done(((f32[2048,1024]{1,0:T(8,128)}), f32[64,1024]{1,0:T(8,128)}) %reduce-scatter.2.cloned.1.call-update) | async-done | bytes 262160 | tf_op jit(solution)/shard_map/reduce_scatter | solution.py:36
  712.1 1.6 convert_element_type.30
Async XLA Ops:
  7.2 132.2 %copy-start = (bf16[1024,512]{1,0:T(8,128)(2,1)S(1)}, bf16[1024,512]{1,0:T(8,128)(2,1)}, u32[]{:S(2)}) copy-start(bf16[1024,512]{1,0:T(8,128)(2,1)} %param.7) | copy-start | bytes 3145732
  7.2 68.5 %all-gather.4.cloned.1.call-start = ((), (), s32[]{:S(2)}) async-start(), calls=%async_computation.1 | async-start | bytes 4325376 | tf_op jit(solution)/shard_map/all_gather | solution.py:27
  7.9 131.5 %all-gather.6.cloned.1.call-start = ((), (), s32[]{:S(2)}) async-start(), calls=%async_computation.2 | async-start | bytes 4325376 | tf_op jit(solution)/shard_map/all_gather | solution.py:21
  8.7 476.3 %all-reduce.3.cloned.1.call-start = ((), (), s32[]{:S(2)}) async-start(), calls=%async_computation.5 | async-start | bytes 16777216 | tf_op jit(solution)/shard_map/psum | solution.py:29
  145.9 407.2 %all-gather.8.cloned.1.call-start = ((), (), s32[]{:S(2)}) async-start(), calls=%async_computation.4 | async-start | bytes 1081344 | tf_op jit(solution)/shard_map/all_gather | solution.py:22
  146.5 565.6 %reduce-scatter.2.cloned.1.call-start = ((), (), s32[]{:S(2)}) async-start(), calls=%async_computation.3 | async-start | bytes 8650752 | tf_op jit(solution)/shard_map/reduce_scatter | solution.py:36
  555.1 5.2 copy-start.1
Sparse Core Ops, SparseCore 0:
  9.9 65.7 all-gather.3
  77.5 61.8 all-gather.5
  146.0 338.8 all-reduce.2
  486.7 66.4 all-gather.7
  555.5 156.4 reduce-scatter.1
where the time goes:
time: 720 us
  waiting for transfers between devices  658 us (91%)
  matrix products  41.8 us (6%)
  between operations  13.8 us (2%)
    psum x1, waiting for transfers between devices, local(): d_hidden = lax.psum(whole_term, 'tp')  338 us
    reduce_scatter x1, waiting for transfers between devices, local(): lax.psum_scatter(partial_input, 'seq', scatter_dimension=0, tiled=True)  136 us
    all_gather x1, waiting for transfers between devices, local(): all_grads = lax.all_gather(out_grad, 'seq', axis=0, tiled=True)  66.9 us
    all_gather x1, waiting for transfers between devices, local(): lax.all_gather(sketch, 'seq', axis=0, tiled=True)  58.2 us
    all_gather x1, waiting for transfers between devices, local(): lax.all_gather(tokens, 'seq', axis=0, tiled=True)  56.9 us
  transfers between devices with their start and end apart: 5, of which 5 were waited for; matrix products, arithmetic and copies ran while one was open for 6% of the time, Pallas kernels for 0%

commit v1 on v0

v1 whole, which is shorter than its diff:
```python
import math

import jax
import jax.numpy as jnp
from jax import lax
from jax.experimental import pallas as pl
from jax.experimental.pallas import tpu as pltpu
from jax.sharding import PartitionSpec as P

MESH = pl.DeviceIdType.MESH
BF16, F32 = jnp.bfloat16, jnp.float32
inv_root_two = 0.7071067811865476
inv_root_twopi = 0.3989422804014327

ROWS, D, FF, SK = 64, 1024, 512, 256
CHUNKS, SLOTS, CH = 4, 8, 512
BLK = 128
WA = D + SK


def dot(a, b):
    return jnp.dot(a, b, preferred_element_type=F32)


class Copies:
    def __init__(self, send, recv):
        self.send, self.recv, self.count, self.started = send, recv, 0, []

    def start(self, src, dst, device):
        i = self.count
        self.count += 1
        copy = pltpu.make_async_remote_copy(
            src_ref=src,
            dst_ref=dst,
            send_sem=self.send.at[i],
            recv_sem=self.recv.at[i],
            device_id=device,
            device_id_type=MESH,
        )
        copy.start()
        self.started.append(copy)
        return copy


N_COPIES = 148
N_LOCAL = 8


def kernel(
    tok_hbm, grd_hbm, win_hbm, wout_hbm, sk_hbm,
    out_hbm, gin_hbm, gout_hbm,
    GA, GB, WI, WO, WIT, WOT, PA, PB, RA, RB, SAF, SBF, SA, SB, ZA, ZB,
    H, DP, DS, DR, OWN, FX, FR, FS, FZ, ACC, SKT, TOKS, GRDS, HS, DPS, SH, OUT, GI, GO,
    send, recv, lsem,
):
    s, t = lax.axis_index("seq"), lax.axis_index("tp")
    c, x, zl = lax.rem(s, 2), lax.rem(s // 2, 4), s // 8
    y, zh = lax.rem(t, 4), t // 4

    def at(zl_, x_, c_):
        return ((zl_ * 4 + x_) * 2 + c_, t)

    def xdev(d):
        return at(zl, lax.rem(x + d, 4), c)

    zpart = [zl, zl + 1 - 2 * lax.rem(zl, 2), lax.rem(zl + 2, 4), 3 - zl]

    def zdev(k):
        return at(zpart[k], x, c)

    def ydev(d):
        return (s, zh * 4 + lax.rem(y + d, 4))

    sib = at(zl, x, 1 - c)
    zhdev = (s, (1 - zh) * 4 + y)

    def slot(c_, d):
        return c_ * 4 + lax.rem(x + d, 4)

    def block(d):
        return pl.ds(pl.multiple_of(lax.rem(y + d, 4) * BLK, BLK), BLK)

    def cols(n):
        return pl.ds(pl.multiple_of(n * 256, 256), 256)

    me = slot(c, 0)
    loads = [
        pltpu.make_async_copy(tok_hbm, GA.at[0, me, :, pl.ds(0, D)], lsem.at[0]),
        pltpu.make_async_copy(sk_hbm, GA.at[0, me, :, pl.ds(D, SK)], lsem.at[1]),
        pltpu.make_async_copy(grd_hbm, GB.at[0, me], lsem.at[2]),
        pltpu.make_async_copy(win_hbm, WI, lsem.at[3]),
        pltpu.make_async_copy(wout_hbm, WO, lsem.at[4]),
    ]
    for load in loads:
        load.start()
    barrier = pltpu.get_barrier_semaphore()
    partners = [sib, zhdev]
    for d in (1, 2, 3):
        partners += [xdev(d), ydev(d), zdev(d)]
    for device in partners:
        pl.semaphore_signal(barrier, inc=1, device_id=device, device_id_type=MESH)
    pl.semaphore_wait(barrier, len(partners))

    copies = Copies(send, recv)
    rc = copies.start
    U = range(8)

    def gat(u):
        return (GA if u < 4 else GB), u % 4

    zin = {}

    def zsend(u):
        G, k = gat(u)
        zin[u] = rc(G.at[0, me], G.at[k, me], zdev(k))

    full, half, sibs = {}, {}, {}

    def ga(u):
        G, k = gat(u)
        if k:
            zin[u].wait_recv()
        own = G.at[k, me]
        full[u] = [rc(own, own, xdev(1)), rc(own, own, xdev(3))]
        sibs[u] = [rc(own, own, sib)]

    def gb(u):
        G, k = gat(u)
        half[u] = []
        for i, (frm, to, r0) in enumerate(((3, 1, 0), (1, 3, ROWS // 2))):
            full[u][i].wait_recv()
            got = G.at[k, slot(c, frm)]
            part = G.at[k, slot(c, frm), pl.ds(r0, ROWS // 2)]
            half[u].append(rc(part, part, xdev(to)))
            sibs[u].append(rc(got, got, sib))

    def gc(u):
        G, k = gat(u)
        for copy in half[u]:
            copy.wait_recv()
        got = G.at[k, slot(c, 2)]
        sibs[u].append(rc(got, got, sib))

    def tokens_of(u):
        G, k = gat(u)
        return G[k, :, :, 0:D].reshape(CH, D)

    ysent = {}

    def m1(u):
        G, k = gat(u)
        for copy in sibs[u]:
            copy.wait_recv()
        W, Pt, R = (WI, PA, RA) if u < 4 else (WOT, PB, RB)

        @pl.loop(0, FF // 256)
        def _(n):
            Pt[k, :, cols(n)] = dot(tokens_of(u), W[:, cols(n)]).astype(BF16)

        ysent[u] = [
            rc(Pt.at[k, :, block(d)], R.at[k, d - 1], ydev(d)) for d in (1, 2, 3)
        ]

    zhsent = {}

    def ysum(u):
        k = u % 4
        Pt, R, SF, S, Z = (PA, RA, SAF, SA, ZA) if u < 4 else (PB, RB, SBF, SB, ZB)
        for copy in ysent[u]:
            copy.wait_recv()
        total = Pt[k, :, block(0)].astype(F32)
        for i in range(3):
            total += R[k, i].astype(F32)
        SF[k] = total
        S[k] = total.astype(BF16)
        zhsent[u] = rc(S.at[k], Z.at[k], zhdev)

    esent = {}

    def zfin(u):
        k = u % 4
        zhsent[u].wait_recv()
        if u < 4:
            v = SAF[k] + ZA[k].astype(F32)
            phi = 0.5 * (1.0 + lax.erf(v * inv_root_two))
            H[k] = (v * phi).astype(BF16)
            SAF[k] = phi + v * jnp.exp(-0.5 * v * v) * inv_root_twopi
        else:
            dh = SBF[k] + ZB[k].astype(F32)
            DP[k, :, block(0)] = (dh * SAF[k]).astype(BF16)
            mine = DP.at[k, :, block(0)]
            esent[k] = [rc(mine, mine, ydev(d)) for d in (1, 2, 3)]

    dsent = {}

    def m2(k):
        for copy in esent[k]:
            copy.wait_recv()
        other = pl.ds(pl.multiple_of((1 - c) * 256, 256), 256)
        own = pl.ds(pl.multiple_of(c * 256, 256), 256)

        @pl.loop(0, D // 256)
        def _(n):
            DS[k, :, cols(n)] = dot(DP[k, other, :], WIT[:, cols(n)]).astype(BF16)

        dsent[k] = rc(DS.at[k], DR.at[k], sib)

        @pl.loop(0, D // 256)
        def _(n):
            OWN[k, :, cols(n)] = dot(DP[k, own, :], WIT[:, cols(n)])

    fsent = {}

    def f1(k):
        dsent[k].wait_recv()
        FX[k] = (OWN[k] + DR[k].astype(F32)).astype(BF16).reshape(4, ROWS, D)
        fsent[k] = [
            rc(FX.at[k, lax.rem(x + d, 4)], FR.at[k, d - 1], xdev(d)) for d in (1, 2, 3)
        ]

    zback = {}

    def f2(k):
        for copy in fsent[k]:
            copy.wait_recv()
        total = FX[k, x].astype(F32)
        for i in range(3):
            total += FR[k, i].astype(F32)
        if k == 0:
            ACC[...] = total
        else:
            FS[k - 1] = total.astype(BF16)
            zback[k] = rc(FS.at[k - 1], FZ.at[k - 1], zdev(k))

    def f3():
        total = ACC[...]
        for k in (1, 2, 3):
            zback[k].wait_recv()
            total += FZ[k - 1].astype(F32)
        OUT[...] = total.astype(BF16)

    def sk_first(k):
        SKT[k] = GA[k, :, :, D : D + SK].reshape(CH, SK).T

    def sk_wide(u, T):
        k = u % 4

        @pl.loop(0, D // 256)
        def _(n):
            G, _k = gat(u)
            part = dot(SKT[k], G[k, :, :, cols(n)].reshape(CH, 256))
            T[:, cols(n)] = part if k == 0 else T[:, cols(n)] + part

    def sk_hid(k):
        part = dot(SKT[k], H[k])
        HS[...] = part if k == 0 else HS[...] + part

    def sk_dpre(k):
        part = dot(SKT[k], DP[k])
        DPS[...] = part if k == 0 else DPS[...] + part

    hsent = []

    def share_hid():
        SH[:, block(0)] = HS[...].astype(BF16)
        mine = SH.at[:, block(0)]
        hsent.extend(rc(mine, mine, ydev(d)) for d in (1, 2, 3))

    scale = 1.0 / math.sqrt(CH * CHUNKS)
    stores = []

    def grad_out():
        for copy in hsent:
            copy.wait_recv()
        left = SH[...].astype(F32).T.astype(BF16)
        WO[...] = (dot(left, GRDS[...].astype(BF16)) * scale).astype(BF16)
        stores.append(pltpu.make_async_copy(WO, gout_hbm, lsem.at[5]))
        stores[-1].start()

    def grad_in():
        left = TOKS[...].T.astype(BF16)
        WI[...] = (dot(left, DPS[...].astype(BF16)) * scale).astype(BF16)
        stores.append(pltpu.make_async_copy(WI, gin_hbm, lsem.at[6]))
        stores[-1].start()

    loads[0].wait()
    loads[1].wait()
    for u in (1, 2, 3):
        zsend(u)
    ga(0)
    loads[2].wait()
    for u in (5, 6, 7):
        zsend(u)
    loads[3].wait()
    loads[4].wait()
    WOT[...] = WO[...].T
    WIT[...] = WI[...].T
    for tick in range(15):
        if tick + 1 in U:
            ga(tick + 1)
        if tick in U:
            gb(tick)
        if tick - 1 in U:
            gc(tick - 1)
        if tick - 2 in U:
            ysum(tick - 2)
        if tick - 1 in U:
            m1(tick - 1)
        if tick - 4 in U:
            zfin(tick - 4)
        if tick - 9 in range(4):
            m2(tick - 9)
        if tick - 10 in range(4):
            f1(tick - 10)
        if tick - 11 in range(4):
            f2(tick - 11)
        if 2 <= tick < 6:
            sk_first(tick - 2)
            sk_wide(tick - 2, TOKS)
        if 5 <= tick < 9:
            sk_hid(tick - 5)
        if tick == 8:
            share_hid()
        if 7 <= tick < 11:
            sk_wide(tick - 3, GRDS)
        if tick == 11:
            grad_out()
        if 9 <= tick < 13:
            sk_dpre(tick - 9)
        if tick == 13:
            grad_in()
    f3()
    stores.append(pltpu.make_async_copy(OUT, out_hbm, lsem.at[7]))
    stores[-1].start()
    for copy in copies.started:
        copy.wait_send()
    for store in stores:
        store.wait()
    assert copies.count <= N_COPIES


def local(tokens, out_grad, w_in, w_out, sketch):
    def vm(*shape, dtype=BF16):
        return pltpu.VMEM(shape, dtype)

    c4 = CHUNKS
    scratch = [
        vm(c4, SLOTS, ROWS, WA), vm(c4, SLOTS, ROWS, D),
        vm(D, FF), vm(FF, D), vm(FF, D), vm(D, FF),
        vm(c4, CH, FF), vm(c4, CH, FF),
        vm(c4, 3, CH, BLK), vm(c4, 3, CH, BLK),
        vm(c4, CH, BLK, dtype=F32), vm(c4, CH, BLK, dtype=F32),
        vm(c4, CH, BLK), vm(c4, CH, BLK), vm(c4, CH, BLK), vm(c4, CH, BLK),
        vm(c4, CH, BLK), vm(c4, CH, FF),
        vm(c4, 256, D), vm(c4, 256, D), vm(c4, 256, D, dtype=F32),
        vm(c4, 4, ROWS, D), vm(c4, 3, ROWS, D),
        vm(3, ROWS, D), vm(3, ROWS, D), vm(ROWS, D, dtype=F32),
        vm(c4, SK, CH),
        vm(SK, D, dtype=F32), vm(SK, D, dtype=F32),
        vm(SK, BLK, dtype=F32), vm(SK, FF, dtype=F32), vm(SK, FF),
        vm(ROWS, D), vm(8, 128), vm(8, 128),
        pltpu.SemaphoreType.DMA((N_COPIES,)),
        pltpu.SemaphoreType.DMA((N_COPIES,)),
        pltpu.SemaphoreType.DMA((N_LOCAL,)),
    ]
    return pl.pallas_call(
        kernel,
        out_shape=(
            jax.ShapeDtypeStruct((ROWS, D), BF16),
            jax.ShapeDtypeStruct((D, FF), BF16),
            jax.ShapeDtypeStruct((FF, D), BF16),
        ),
        in_specs=[pl.BlockSpec(memory_space=pl.ANY)] * 5,
        out_specs=[pl.BlockSpec(memory_space=pl.ANY)] * 3,
        scratch_shapes=scratch,
        compiler_params=pltpu.CompilerParams(
            collective_id=0, has_side_effects=True, vmem_limit_bytes=60 << 20
        ),
        cost_estimate=pl.CostEstimate(
            flops=10 * 10**9, bytes_accessed=6 * 2**20, transcendentals=2**19
        ),
        name="ffn_grads",
    )(tokens, out_grad, w_in, w_out, sketch)


def solution(mesh):
    return jax.shard_map(
        local,
        mesh=mesh,
        in_specs=(P("seq", "tp"), P("seq", "tp"), P("tp", "seq"), P("seq", "tp"), P("seq", None)),
        out_specs=(P("seq", "tp"), P("tp", "seq"), P("seq", "tp")),
        check_vma=False,
    )
```

time: 720 us -> 152 us (0.21)
  waiting for transfers between devices: 658 us -> 0 us
  Pallas kernels: 0 us -> 144 us
  matrix products: 41.8 us -> 0 us
  between operations: 13.8 us -> 0.64 us
    psum x1 -> x0, waiting for transfers between devices: 338 us -> none  [local(): d_hidden = lax.psum(whole_term, 'tp')]
    all_gather x3 -> x0, waiting for transfers between devices: 182 us -> none  [the longest x1 66.9 us: local(): all_grads = lax.all_gather(out_grad, 'seq', axis=0, tiled=True)]
    pallas_call x0 -> x1, Pallas kernels: none -> 144 us  [local(): pl.pallas_call(kernel, out_shape=(jax.ShapeDtypeStruct((ROWS, D), BF16),...]
    reduce_scatter x1 -> x0, waiting for transfers between devices: 136 us -> none  [local(): lax.psum_scatter(partial_input, 'seq', scatter_dimension=0, tiled=True)]
    dot_general x7 -> x0, matrix products: 41.8 us -> none  [the longest x1 10.9 us: local(): jnp.einsum('tr,tf->rf', all_sketch, hidden, preferred_element_type=jnp.fl...]
  transfers between devices with their start and end apart: 5 -> 0, of which waited for: 5 -> 0; matrix products, arithmetic and copies ran while one was open for 6% -> 0% of each run, Pallas kernels for 0% -> 0%
where the time goes in v1:
time: 152 us; the launch traced here: 149 us
  Pallas kernels  144 us (95%)
  local copies, waits for them, and re-layouts  4.89 us (3%)
    pallas_call x1, Pallas kernels, local(): pl.pallas_call(kernel, out_shape=(jax.ShapeDtypeStruct((ROWS, D), BF16),...  144 us
    unnamed x5, local copies, waits for them, and re-layouts  4.89 us

profile of v1, /device:TPU:8, one launch (start us, length us, event | category | flops | bytes accessed | tf_op | source)
XLA Modules:
  0.0 149.2 jit_solution(12416112105411154364)
XLA Ops:
  0.6 143.7 %ffn_grads.1 = (bf16[64,1024]{1,0:T(8,128)(2,1)}, bf16[1024,512]{1,0:T(8,128)(2,1)}, bf16[512,1024]{1,0:T(8,128)(2,1)}) custom-call(bf16[64,1024]{1,0:T(8,128)(2,1)} %tok_hbm.1, bf16[64,1024]{1,0:T(8,128)(2,1)} %grd_hbm.1, bf16[1024,512]{1,0:T(8,128)(2,1)} %win_hbm.1, bf16[512,1024]{1,0:T(8,128)(2,1)} %wout_hbm.1, bf16[64,256]{1,0:T(8,128)(2,1)} %sk_hbm.1), custom_call_target="tpu_custom_call" | custom-call | flops 10000000000 | bytes 6291456 | tf_op jit(solution)/shard_map/ffn_grads/pallas_call | solution.py:366
  144.3 1.6 %copy.11 = bf16[64,1024]{1,0:T(8,128)(2,1)} copy(bf16[64,1024]{1,0:T(8,128)(2,1)} %get-tuple-element.6) | data formatting | bytes 262144
  145.9 0.0 copy-start
  145.9 2.4 %copy.12 = bf16[1024,512]{1,0:T(8,128)(2,1)} copy(bf16[1024,512]{1,0:T(8,128)(2,1)} %get-tuple-element.7) | data formatting | bytes 2097152
  148.2 0.0 copy-done
  148.2 1.0 copy.13
Async XLA Ops:
  145.9 2.4 %copy-start = (bf16[512,1024]{1,0:T(8,128)(2,1)S(1)}, bf16[512,1024]{1,0:T(8,128)(2,1)}, u32[]{:S(2)}) copy-start(bf16[512,1024]{1,0:T(8,128)(2,1)} %get-tuple-element.8) | copy-start | bytes 3145732

commit v2 on v1

--- a/solution.py
+++ b/solution.py
@@ -16,6 +16,8 @@
 CHUNKS, SLOTS, CH = 4, 8, 512
 BLK = 128
 WA = D + SK
+LO, HI = pl.ds(0, CH // 2), pl.ds(CH // 2, CH // 2)
+TOP, BOT = pl.ds(0, ROWS // 2), pl.ds(ROWS // 2, ROWS // 2)
 
 
 def dot(a, b):
@@ -42,15 +44,33 @@
         return copy
 
 
-N_COPIES = 148
+N_COPIES = 200
 N_LOCAL = 8
+
+SCHEDULE = (
+    ("start", 0), ("ga", 0), ("ga", 4), ("weights", 0), ("gb", 0), ("ga", 1), ("gb", 4),
+    ("ga", 5), ("gc", 0), ("m1", 0), ("skf", 0), ("gb", 1), ("skt", 0), ("gc", 4), ("ga", 2),
+    ("ymid", 0), ("m1", 4), ("gb", 5), ("skg", 0), ("gc", 1), ("ysum", 0), ("ga", 6), ("ymid", 4),
+    ("m1", 1), ("gb", 2), ("gc", 5), ("skf", 1), ("ysum", 4), ("m1", 5), ("gb", 6), ("ymid", 1),
+    ("gc", 2), ("ga", 3), ("skg", 1), ("skt", 1), ("ymid", 5), ("gc", 6), ("m1", 2), ("m1", 6),
+    ("ysum", 1), ("gb", 3), ("ysum", 5), ("skf", 2), ("ymid", 2), ("zfin", 0), ("ga", 7),
+    ("gc", 3), ("ymid", 6), ("zfin", 4), ("m1", 3), ("ysum", 2), ("zfin", 1), ("gb", 7),
+    ("ysum", 6), ("skf", 3), ("zfin", 5), ("ymid", 3), ("gc", 7), ("skg", 2), ("skh", 0),
+    ("ey", 0), ("m1", 7), ("skg", 3), ("skh", 1), ("zfin", 2), ("ysum", 3), ("efwd", 0),
+    ("skh", 2), ("skt", 2), ("ymid", 7), ("zfin", 6), ("skt", 3), ("ey", 1), ("m2", 0),
+    ("ysum", 7), ("skd", 0), ("zfin", 3), ("f1", 0), ("efwd", 1), ("skh", 3), ("hz", 3),
+    ("ey", 2), ("zfin", 7), ("fmid", 0), ("m2", 1), ("efwd", 2), ("skd", 1), ("hy", 3), ("f1", 1),
+    ("f2", 0), ("ey", 3), ("m2", 2), ("fmid", 1), ("skd", 2), ("f1", 2), ("efwd", 3), ("go", 3),
+    ("f2", 1), ("fmid", 2), ("m2", 3), ("skd", 3), ("gi", 3), ("f1", 3), ("f2", 2), ("fmid", 3),
+    ("f2", 3),
+)
 
 
 def kernel(
     tok_hbm, grd_hbm, win_hbm, wout_hbm, sk_hbm,
     out_hbm, gin_hbm, gout_hbm,
     GA, GB, WI, WO, WIT, WOT, PA, PB, RA, RB, SAF, SBF, SA, SB, ZA, ZB,
-    H, DP, DS, DR, OWN, FX, FR, FS, FZ, ACC, SKT, TOKS, GRDS, HS, DPS, SH, OUT, GI, GO,
+    H, DP, DS, DR, OWN, FX, FR, FS, FZ, ACC, SKT, TOKS, GRDS, HS, HB, HZ, DPS, SH, OUT,
     send, recv, lsem,
 ):
     s, t = lax.axis_index("seq"), lax.axis_index("tp")
@@ -76,6 +96,9 @@
 
     def slot(c_, d):
         return c_ * 4 + lax.rem(x + d, 4)
+
+    def xrow(d):
+        return lax.rem(x + d, 4)
 
     def block(d):
         return pl.ds(pl.multiple_of(lax.rem(y + d, 4) * BLK, BLK), BLK)
@@ -157,25 +180,43 @@
         def _(n):
             Pt[k, :, cols(n)] = dot(tokens_of(u), W[:, cols(n)]).astype(BF16)
 
+        two, up, down = Pt.at[k, :, block(2)], ydev(1), ydev(3)
         ysent[u] = [
-            rc(Pt.at[k, :, block(d)], R.at[k, d - 1], ydev(d)) for d in (1, 2, 3)
+            rc(two.at[LO], R.at[k, 2, LO], up),
+            rc(two.at[HI], R.at[k, 2, HI], down),
+            rc(Pt.at[k, HI, block(1)], R.at[k, 0, HI], up),
+            rc(Pt.at[k, LO, block(3)], R.at[k, 1, LO], down),
         ]
 
+    def ymid(u):
+        k = u % 4
+        Pt, R = (PA, RA) if u < 4 else (PB, RB)
+        for i, (d, half_, to) in enumerate(((1, LO, 0), (3, HI, 1))):
+            ysent[u][i].wait_recv()
+            Pt[k, half_, block(d)] = (
+                Pt[k, half_, block(d)].astype(F32) + R[k, 2, half_].astype(F32)
+            ).astype(BF16)
+            ysent[u].append(rc(Pt.at[k, half_, block(d)], R.at[k, to, half_], ydev(d)))
+
     zhsent = {}
+    mine_z = pl.ds(pl.multiple_of(zh * (CH // 2), CH // 2), CH // 2)
+    theirs_z = pl.ds(pl.multiple_of((1 - zh) * (CH // 2), CH // 2), CH // 2)
 
     def ysum(u):
         k = u % 4
         Pt, R, SF, S, Z = (PA, RA, SAF, SA, ZA) if u < 4 else (PB, RB, SBF, SB, ZB)
-        for copy in ysent[u]:
-            copy.wait_recv()
-        total = Pt[k, :, block(0)].astype(F32)
-        for i in range(3):
-            total += R[k, i].astype(F32)
-        SF[k] = total
-        S[k] = total.astype(BF16)
+        for copy in ysent[u][2:]:
+            copy.wait_recv()
+
+        def total(rows):
+            own = Pt[k, rows, block(0)].astype(F32)
+            return own + R[k, 0, rows].astype(F32) + R[k, 1, rows].astype(F32)
+
+        S[k] = total(theirs_z).astype(BF16)
         zhsent[u] = rc(S.at[k], Z.at[k], zhdev)
-
-    esent = {}
+        SF[k] = total(mine_z)
+
+    esent, ezsent = {}, {}
 
     def zfin(u):
         k = u % 4
@@ -187,14 +228,27 @@
             SAF[k] = phi + v * jnp.exp(-0.5 * v * v) * inv_root_twopi
         else:
             dh = SBF[k] + ZB[k].astype(F32)
-            DP[k, :, block(0)] = (dh * SAF[k]).astype(BF16)
-            mine = DP.at[k, :, block(0)]
-            esent[k] = [rc(mine, mine, ydev(d)) for d in (1, 2, 3)]
+            DP[k, mine_z, block(0)] = (dh * SAF[k]).astype(BF16)
+            mine = DP.at[k, mine_z, block(0)]
+            ezsent[k] = rc(mine, mine, zhdev)
+            esent[k] = [rc(mine, mine, ydev(d)) for d in (1, 3)]
+
+    def ey(k):
+        ezsent[k].wait_recv()
+        theirs = DP.at[k, theirs_z, block(0)]
+        esent[k] += [rc(theirs, theirs, ydev(d)) for d in (1, 3)]
+
+    def efwd(k):
+        for i, (frm, to, half_) in enumerate(((3, 1, LO), (1, 3, HI))):
+            esent[k][i].wait_recv()
+            esent[k][2 + i].wait_recv()
+            part = DP.at[k, half_, block(frm)]
+            esent[k].append(rc(part, part, ydev(to)))
 
     dsent = {}
 
     def m2(k):
-        for copy in esent[k]:
+        for copy in esent[k][4:]:
             copy.wait_recv()
         other = pl.ds(pl.multiple_of((1 - c) * 256, 256), 256)
         own = pl.ds(pl.multiple_of(c * 256, 256), 256)
@@ -214,17 +268,29 @@
     def f1(k):
         dsent[k].wait_recv()
         FX[k] = (OWN[k] + DR[k].astype(F32)).astype(BF16).reshape(4, ROWS, D)
+        two, up, down = xrow(2), xdev(1), xdev(3)
         fsent[k] = [
-            rc(FX.at[k, lax.rem(x + d, 4)], FR.at[k, d - 1], xdev(d)) for d in (1, 2, 3)
+            rc(FX.at[k, two, TOP], FR.at[k, 2, TOP], up),
+            rc(FX.at[k, two, BOT], FR.at[k, 2, BOT], down),
+            rc(FX.at[k, xrow(1), BOT], FR.at[k, 0, BOT], up),
+            rc(FX.at[k, xrow(3), TOP], FR.at[k, 1, TOP], down),
         ]
 
+    def fmid(k):
+        for i, (d, half_, to) in enumerate(((1, TOP, 0), (3, BOT, 1))):
+            fsent[k][i].wait_recv()
+            FX[k, xrow(d), half_] = (
+                FX[k, xrow(d), half_].astype(F32) + FR[k, 2, half_].astype(F32)
+            ).astype(BF16)
+            fsent[k].append(rc(FX.at[k, xrow(d), half_], FR.at[k, to, half_], xdev(d)))
+
     zback = {}
 
     def f2(k):
-        for copy in fsent[k]:
+        for copy in fsent[k][2:]:
             copy.wait_recv()
         total = FX[k, x].astype(F32)
-        for i in range(3):
+        for i in range(2):
             total += FR[k, i].astype(F32)
         if k == 0:
             ACC[...] = total
@@ -252,7 +318,7 @@
             T[:, cols(n)] = part if k == 0 else T[:, cols(n)] + part
 
     def sk_hid(k):
-        part = dot(SKT[k], H[k])
+        part = dot(SKT[k, :, mine_z], H[k])
         HS[...] = part if k == 0 else HS[...] + part
 
     def sk_dpre(k):
@@ -261,8 +327,13 @@
 
     hsent = []
 
-    def share_hid():
-        SH[:, block(0)] = HS[...].astype(BF16)
+    def hid_z(k):
+        HB[...] = HS[...].astype(BF16)
+        hsent.append(rc(HB, HZ, zhdev))
+
+    def hid_y(k):
+        hsent.pop().wait_recv()
+        SH[:, block(0)] = (HS[...] + HZ[...].astype(F32)).astype(BF16)
         mine = SH.at[:, block(0)]
         hsent.extend(rc(mine, mine, ydev(d)) for d in (1, 2, 3))
 
@@ -283,52 +354,27 @@
         stores.append(pltpu.make_async_copy(WI, gin_hbm, lsem.at[6]))
         stores[-1].start()
 
-    loads[0].wait()
-    loads[1].wait()
-    for u in (1, 2, 3):
-        zsend(u)
-    ga(0)
-    loads[2].wait()
-    for u in (5, 6, 7):
-        zsend(u)
-    loads[3].wait()
-    loads[4].wait()
-    WOT[...] = WO[...].T
-    WIT[...] = WI[...].T
-    for tick in range(15):
-        if tick + 1 in U:
-            ga(tick + 1)
-        if tick in U:
-            gb(tick)
-        if tick - 1 in U:
-            gc(tick - 1)
-        if tick - 2 in U:
-            ysum(tick - 2)
-        if tick - 1 in U:
-            m1(tick - 1)
-        if tick - 4 in U:
-            zfin(tick - 4)
-        if tick - 9 in range(4):
-            m2(tick - 9)
-        if tick - 10 in range(4):
-            f1(tick - 10)
-        if tick - 11 in range(4):
-            f2(tick - 11)
-        if 2 <= tick < 6:
-            sk_first(tick - 2)
-            sk_wide(tick - 2, TOKS)
-        if 5 <= tick < 9:
-            sk_hid(tick - 5)
-        if tick == 8:
-            share_hid()
-        if 7 <= tick < 11:
-            sk_wide(tick - 3, GRDS)
-        if tick == 11:
-            grad_out()
-        if 9 <= tick < 13:
-            sk_dpre(tick - 9)
-        if tick == 13:
-            grad_in()
+    def start(_):
+        loads[0].wait()
+        loads[1].wait()
+        loads[2].wait()
+        for u in (1, 5, 2, 6, 3, 7):
+            zsend(u)
+
+    def weights(_):
+        loads[3].wait()
+        loads[4].wait()
+        WOT[...] = WO[...].T
+        WIT[...] = WI[...].T
+
+    stages = dict(
+        start=start, weights=weights, ga=ga, gb=gb, gc=gc, m1=m1, ymid=ymid, ysum=ysum, zfin=zfin,
+        ey=ey, efwd=efwd, m2=m2, f1=f1, fmid=fmid, f2=f2, skf=sk_first,
+        skt=lambda k: sk_wide(k, TOKS), skg=lambda k: sk_wide(k + 4, GRDS), skh=sk_hid,
+        skd=sk_dpre, hz=hid_z, hy=hid_y, go=lambda k: grad_out(), gi=lambda k: grad_in(),
+    )
+    for name, arg in SCHEDULE:
+        stages[name](arg)
     f3()
     stores.append(pltpu.make_async_copy(OUT, out_hbm, lsem.at[7]))
     stores[-1].start()
@@ -349,16 +395,18 @@
         vm(D, FF), vm(FF, D), vm(FF, D), vm(D, FF),
         vm(c4, CH, FF), vm(c4, CH, FF),
         vm(c4, 3, CH, BLK), vm(c4, 3, CH, BLK),
-        vm(c4, CH, BLK, dtype=F32), vm(c4, CH, BLK, dtype=F32),
-        vm(c4, CH, BLK), vm(c4, CH, BLK), vm(c4, CH, BLK), vm(c4, CH, BLK),
-        vm(c4, CH, BLK), vm(c4, CH, FF),
+        vm(c4, CH // 2, BLK, dtype=F32), vm(c4, CH // 2, BLK, dtype=F32),
+        vm(c4, CH // 2, BLK), vm(c4, CH // 2, BLK),
+        vm(c4, CH // 2, BLK), vm(c4, CH // 2, BLK),
+        vm(c4, CH // 2, BLK), vm(c4, CH, FF),
         vm(c4, 256, D), vm(c4, 256, D), vm(c4, 256, D, dtype=F32),
         vm(c4, 4, ROWS, D), vm(c4, 3, ROWS, D),
         vm(3, ROWS, D), vm(3, ROWS, D), vm(ROWS, D, dtype=F32),
         vm(c4, SK, CH),
         vm(SK, D, dtype=F32), vm(SK, D, dtype=F32),
-        vm(SK, BLK, dtype=F32), vm(SK, FF, dtype=F32), vm(SK, FF),
-        vm(ROWS, D), vm(8, 128), vm(8, 128),
+        vm(SK, BLK, dtype=F32), vm(SK, BLK), vm(SK, BLK),
+        vm(SK, FF, dtype=F32), vm(SK, FF),
+        vm(ROWS, D),
         pltpu.SemaphoreType.DMA((N_COPIES,)),
         pltpu.SemaphoreType.DMA((N_COPIES,)),
         pltpu.SemaphoreType.DMA((N_LOCAL,)),

time: 152 us -> 118 us (0.78); the launches traced: 149 us -> 117 us
  Pallas kernels: 144 us -> 112 us
    pallas_call x1, Pallas kernels: 144 us -> 112 us  [local(): pl.pallas_call(kernel, out_shape=(jax.ShapeDtypeStruct((ROWS, D), BF16),...]
where the time goes in v2:
time: 118 us; the launch traced here: 117 us
  Pallas kernels  112 us (95%)
  local copies, waits for them, and re-layouts  4.89 us (4%)
    pallas_call x1, Pallas kernels, local(): pl.pallas_call(kernel, out_shape=(jax.ShapeDtypeStruct((ROWS, D), BF16),...  112 us
    unnamed x5, local copies, waits for them, and re-layouts  4.89 us

profile of v2, /device:TPU:8, one launch (start us, length us, event | category | flops | bytes accessed | tf_op | source)
XLA Modules:
  0.0 117.1 jit_solution(14742565389727714020)
XLA Ops:
  0.6 111.6 %ffn_grads.1 = (bf16[64,1024]{1,0:T(8,128)(2,1)}, bf16[1024,512]{1,0:T(8,128)(2,1)}, bf16[512,1024]{1,0:T(8,128)(2,1)}) custom-call(bf16[64,1024]{1,0:T(8,128)(2,1)} %tok_hbm.1, bf16[64,1024]{1,0:T(8,128)(2,1)} %grd_hbm.1, bf16[1024,512]{1,0:T(8,128)(2,1)} %win_hbm.1, bf16[512,1024]{1,0:T(8,128)(2,1)} %wout_hbm.1, bf16[64,256]{1,0:T(8,128)(2,1)} %sk_hbm.1), custom_call_target="tpu_custom_call" | custom-call | flops 10000000000 | bytes 6291456 | tf_op jit(solution)/shard_map/ffn_grads/pallas_call | solution.py:414
  112.2 1.6 %copy.11 = bf16[64,1024]{1,0:T(8,128)(2,1)} copy(bf16[64,1024]{1,0:T(8,128)(2,1)} %get-tuple-element.6) | data formatting | bytes 262144
  113.8 0.0 copy-start
  113.8 2.4 %copy.12 = bf16[1024,512]{1,0:T(8,128)(2,1)} copy(bf16[1024,512]{1,0:T(8,128)(2,1)} %get-tuple-element.7) | data formatting | bytes 2097152
  116.1 0.0 copy-done
  116.1 1.0 copy.13
Async XLA Ops:
  113.8 2.4 %copy-start = (bf16[512,1024]{1,0:T(8,128)(2,1)S(1)}, bf16[512,1024]{1,0:T(8,128)(2,1)}, u32[]{:S(2)}) copy-start(bf16[512,1024]{1,0:T(8,128)(2,1)} %get-tuple-element.8) | copy-start | bytes 3145732

commit v3 on v2

--- a/solution.py
+++ b/solution.py
@@ -70,7 +70,7 @@
     tok_hbm, grd_hbm, win_hbm, wout_hbm, sk_hbm,
     out_hbm, gin_hbm, gout_hbm,
     GA, GB, WI, WO, WIT, WOT, PA, PB, RA, RB, SAF, SBF, SA, SB, ZA, ZB,
-    H, DP, DS, DR, OWN, FX, FR, FS, FZ, ACC, SKT, TOKS, GRDS, HS, HB, HZ, DPS, SH, OUT,
+    H, DP, DS, DR, FX, FR, FS, FZ, ACC, SKT, TOKS, GRDS, HS, HB, HZ, DPS, SH, OUT,
     send, recv, lsem,
 ):
     s, t = lax.axis_index("seq"), lax.axis_index("tp")
@@ -246,28 +246,24 @@
             esent[k].append(rc(part, part, ydev(to)))
 
     dsent = {}
+    mine_c = pl.ds(pl.multiple_of(c * (CH // 2), CH // 2), CH // 2)
+    theirs_c = pl.ds(pl.multiple_of((1 - c) * (CH // 2), CH // 2), CH // 2)
 
     def m2(k):
         for copy in esent[k][4:]:
             copy.wait_recv()
-        other = pl.ds(pl.multiple_of((1 - c) * 256, 256), 256)
-        own = pl.ds(pl.multiple_of(c * 256, 256), 256)
 
         @pl.loop(0, D // 256)
         def _(n):
-            DS[k, :, cols(n)] = dot(DP[k, other, :], WIT[:, cols(n)]).astype(BF16)
-
-        dsent[k] = rc(DS.at[k], DR.at[k], sib)
-
-        @pl.loop(0, D // 256)
-        def _(n):
-            OWN[k, :, cols(n)] = dot(DP[k, own, :], WIT[:, cols(n)])
+            DS[k, :, cols(n)] = dot(DP[k], WIT[:, cols(n)]).astype(BF16)
+
+        dsent[k] = rc(DS.at[k, theirs_c], DR.at[k], sib)
 
     fsent = {}
 
     def f1(k):
         dsent[k].wait_recv()
-        FX[k] = (OWN[k] + DR[k].astype(F32)).astype(BF16).reshape(4, ROWS, D)
+        FX[k] = (DS[k, mine_c].astype(F32) + DR[k].astype(F32)).astype(BF16).reshape(4, ROWS, D)
         two, up, down = xrow(2), xdev(1), xdev(3)
         fsent[k] = [
             rc(FX.at[k, two, TOP], FR.at[k, 2, TOP], up),
@@ -385,6 +381,24 @@
     assert copies.count <= N_COPIES
 
 
+def hand_on(a, b, c, a_out, b_out, c_out, a_buf, b_buf, c_buf, sems):
+    parts = [(b, b_buf, b_out, i) for i in range(4)] + [(c, c_buf, c_out, i) for i in range(4)]
+    loads, stores = [], []
+    for n, (src, buf, dst, i) in enumerate(parts + [(a, a_buf, a_out, None)]):
+        if i is not None:
+            rows = src.shape[0] // 4
+            src, buf, dst = (r.at[pl.ds(i * rows, rows)] for r in (src, buf, dst))
+        loads.append(pltpu.make_async_copy(src, buf, sems.at[0, n]))
+        stores.append(pltpu.make_async_copy(buf, dst, sems.at[1, n]))
+    for load in loads:
+        load.start()
+    for load, store in zip(loads, stores):
+        load.wait()
+        store.start()
+    for store in stores:
+        store.wait()
+
+
 def local(tokens, out_grad, w_in, w_out, sketch):
     def vm(*shape, dtype=BF16):
         return pltpu.VMEM(shape, dtype)
@@ -399,7 +413,7 @@
         vm(c4, CH // 2, BLK), vm(c4, CH // 2, BLK),
         vm(c4, CH // 2, BLK), vm(c4, CH // 2, BLK),
         vm(c4, CH // 2, BLK), vm(c4, CH, FF),
-        vm(c4, 256, D), vm(c4, 256, D), vm(c4, 256, D, dtype=F32),
+        vm(c4, CH, D), vm(c4, CH // 2, D),
         vm(c4, 4, ROWS, D), vm(c4, 3, ROWS, D),
         vm(3, ROWS, D), vm(3, ROWS, D), vm(ROWS, D, dtype=F32),
         vm(c4, SK, CH),
@@ -411,7 +425,7 @@
         pltpu.SemaphoreType.DMA((N_COPIES,)),
         pltpu.SemaphoreType.DMA((N_LOCAL,)),
     ]
-    return pl.pallas_call(
+    results = pl.pallas_call(
         kernel,
         out_shape=(
             jax.ShapeDtypeStruct((ROWS, D), BF16),
@@ -429,6 +443,14 @@
         ),
         name="ffn_grads",
     )(tokens, out_grad, w_in, w_out, sketch)
+    return pl.pallas_call(
+        hand_on,
+        out_shape=tuple(jax.ShapeDtypeStruct(r.shape, r.dtype) for r in results),
+        in_specs=[pl.BlockSpec(memory_space=pl.ANY)] * 3,
+        out_specs=[pl.BlockSpec(memory_space=pl.ANY)] * 3,
+        scratch_shapes=[vm(*r.shape) for r in results] + [pltpu.SemaphoreType.DMA((2, 9))],
+        name="hand_on",
+    )(*results)
 
 
 def solution(mesh):

time: 118 us -> 115 us (0.975)
  local copies, waits for them, and re-layouts: 4.89 us -> 0 us
  Pallas kernels: 112 us -> 114 us
    unnamed x5 -> x0, local copies, waits for them, and re-layouts: 4.89 us -> none
    pallas_call x0 -> x1, Pallas kernels: none -> 2.45 us  [local(): pl.pallas_call(hand_on, out_shape=tuple((jax.ShapeDtypeStruct(r.shape, r....]
where the time goes in v3:
time: 115 us
  Pallas kernels  114 us (99%)
    pallas_call x1, Pallas kernels, local(): pl.pallas_call(kernel, out_shape=(jax.ShapeDtypeStruct((ROWS, D), BF16),...  112 us
    pallas_call x1, Pallas kernels, local(): pl.pallas_call(hand_on, out_shape=tuple((jax.ShapeDtypeStruct(r.shape, r....  2.45 us

profile of v3, /device:TPU:8, one launch (start us, length us, event | category | flops | bytes accessed | tf_op | source)
XLA Modules:
  0.0 114.7 jit_solution(4949860240707685623)
XLA Ops:
  0.6 111.7 %ffn_grads.1 = (bf16[64,1024]{1,0:T(8,128)(2,1)}, bf16[1024,512]{1,0:T(8,128)(2,1)}, bf16[512,1024]{1,0:T(8,128)(2,1)}) custom-call(bf16[64,1024]{1,0:T(8,128)(2,1)} %tok_hbm.1, bf16[64,1024]{1,0:T(8,128)(2,1)} %grd_hbm.1, bf16[1024,512]{1,0:T(8,128)(2,1)} %win_hbm.1, bf16[512,1024]{1,0:T(8,128)(2,1)} %wout_hbm.1, bf16[64,256]{1,0:T(8,128)(2,1)} %sk_hbm.1), custom_call_target="tpu_custom_call" | custom-call | flops 10000000000 | bytes 6291456 | tf_op jit(solution)/shard_map/ffn_grads/pallas_call | solution.py:428
  112.3 2.5 %hand_on.1 = (bf16[64,1024]{1,0:T(8,128)(2,1)}, bf16[1024,512]{1,0:T(8,128)(2,1)}, bf16[512,1024]{1,0:T(8,128)(2,1)}) custom-call(bf16[64,1024]{1,0:T(8,128)(2,1)} %get-tuple-element.6.a, bf16[1024,512]{1,0:T(8,128)(2,1)} %get-tuple-element.7.b, bf16[512,1024]{1,0:T(8,128)(2,1)} %get-tuple-element.8.c), custom_call_target="tpu_custom_call" | custom-call | tf_op jit(solution)/shard_map/hand_on/pallas_call | solution.py:446

commit v4 on v3

--- a/solution.py
+++ b/solution.py
@@ -44,7 +44,7 @@
         return copy
 
 
-N_COPIES = 200
+N_COPIES = 220
 N_LOCAL = 8
 
 SCHEDULE = (
@@ -144,7 +144,13 @@
         if k:
             zin[u].wait_recv()
         own = G.at[k, me]
-        full[u] = [rc(own, own, xdev(1)), rc(own, own, xdev(3))]
+        top, bottom = G.at[k, me, TOP], G.at[k, me, BOT]
+        full[u] = [
+            rc(top, top, xdev(1)),
+            rc(bottom, bottom, xdev(3)),
+            rc(bottom, bottom, xdev(1)),
+            rc(top, top, xdev(3)),
+        ]
         sibs[u] = [rc(own, own, sib)]
 
     def gb(u):
@@ -152,9 +158,11 @@
         half[u] = []
         for i, (frm, to, r0) in enumerate(((3, 1, 0), (1, 3, ROWS // 2))):
             full[u][i].wait_recv()
-            got = G.at[k, slot(c, frm)]
             part = G.at[k, slot(c, frm), pl.ds(r0, ROWS // 2)]
             half[u].append(rc(part, part, xdev(to)))
+        for i, frm in enumerate((3, 1)):
+            full[u][2 + i].wait_recv()
+            got = G.at[k, slot(c, frm)]
             sibs[u].append(rc(got, got, sib))
 
     def gc(u):
@@ -176,14 +184,18 @@
             copy.wait_recv()
         W, Pt, R = (WI, PA, RA) if u < 4 else (WOT, PB, RB)
 
-        @pl.loop(0, FF // 256)
-        def _(n):
+        def columns(n):
             Pt[k, :, cols(n)] = dot(tokens_of(u), W[:, cols(n)]).astype(BF16)
 
         two, up, down = Pt.at[k, :, block(2)], ydev(1), ydev(3)
+        first = lax.rem(y + 2, 4) // 2
+        columns(first)
         ysent[u] = [
             rc(two.at[LO], R.at[k, 2, LO], up),
             rc(two.at[HI], R.at[k, 2, HI], down),
+        ]
+        columns(1 - first)
+        ysent[u] += [
             rc(Pt.at[k, HI, block(1)], R.at[k, 0, HI], up),
             rc(Pt.at[k, LO, block(3)], R.at[k, 1, LO], down),
         ]

time: 115 us -> 114 us (level)
  no operation moved by 1% of the time
where the time goes in v4:
time: 114 us
  Pallas kernels  113 us (99%)
    pallas_call x1, Pallas kernels, local(): pl.pallas_call(kernel, out_shape=(jax.ShapeDtypeStruct((ROWS, D), BF16),...  111 us
    pallas_call x1, Pallas kernels, local(): pl.pallas_call(hand_on, out_shape=tuple((jax.ShapeDtypeStruct(r.shape, r....  2.45 us

profile of v4, /device:TPU:8, one launch (start us, length us, event | category | flops | bytes accessed | tf_op | source)
XLA Modules:
  0.0 114.0 jit_solution(18079921834539978620)
XLA Ops:
  0.6 110.9 %ffn_grads.1 = (bf16[64,1024]{1,0:T(8,128)(2,1)}, bf16[1024,512]{1,0:T(8,128)(2,1)}, bf16[512,1024]{1,0:T(8,128)(2,1)}) custom-call(bf16[64,1024]{1,0:T(8,128)(2,1)} %tok_hbm.1, bf16[64,1024]{1,0:T(8,128)(2,1)} %grd_hbm.1, bf16[1024,512]{1,0:T(8,128)(2,1)} %win_hbm.1, bf16[512,1024]{1,0:T(8,128)(2,1)} %wout_hbm.1, bf16[64,256]{1,0:T(8,128)(2,1)} %sk_hbm.1), custom_call_target="tpu_custom_call" | custom-call | flops 10000000000 | bytes 6291456 | tf_op jit(solution)/shard_map/ffn_grads/pallas_call | solution.py:440
  111.5 2.5 %hand_on.1 = (bf16[64,1024]{1,0:T(8,128)(2,1)}, bf16[1024,512]{1,0:T(8,128)(2,1)}, bf16[512,1024]{1,0:T(8,128)(2,1)}) custom-call(bf16[64,1024]{1,0:T(8,128)(2,1)} %get-tuple-element.6.a, bf16[1024,512]{1,0:T(8,128)(2,1)} %get-tuple-element.7.b, bf16[512,1024]{1,0:T(8,128)(2,1)} %get-tuple-element.8.c), custom_call_target="tpu_custom_call" | custom-call | tf_op jit(solution)/shard_map/hand_on/pallas_call | solution.py:458
